TPU v7x, 32 devices: a whole 2x2x4 slice. The times are simulated.
32 devices in a mesh: groups: 2 (over y), tok: 4 (over z), col: 4 (over x, core).
Axes of the slice: x: 2, y: 2, z: 4, core: 2. Of those that a mesh axis runs over, the one named last changes fastest.
Arguments:
- attn_out: bfloat16 [512, 8192], P(('groups', 'tok'), 'col'), parts along dimension 0, may hold values from -12 to 12
- residual: bfloat16 [512, 8192], P(('groups', 'col'), 'tok'), parts along dimension 0, may hold values from -310 to 310
- w_out: bfloat16 [8192, 8192], P('col', 'tok'), may hold values from -0.0625 to 0.0625
- norm_gain: float32 [8192], P('tok'), may hold values from 0.5 to 1.5
- rotation: bfloat16 [8192, 8192], P('tok', 'col'), may hold values from -0.23201941 to 0.23201941
Outputs:
- kurtosis: float32 [512], P(('groups', 'tok')), parts along dimension 0
- grad_rot: float32 [16384, 8192], P(('groups', 'tok'), 'col'), parts along dimension 0
There are 2 independent parts, one for each index of `groups`. A program takes and returns all parts, laid end to end along the dimension named above; an argument that names none is the same for every part. Nothing has to cross between parts.
All inputs are finite; a program needn't handle non-finite values.
Results may differ from a plain program's by a relative error of at most 0.0018.
The roundings to bfloat16 on the way count: a program that leaves them out, or rounds other values in their place, can miss the bound.
Values may be sent and summed in bfloat16 or wider, within the bound.
A program may use at most 128 MiB of HBM per device.

v0:
```python
import math
import jax
import jax.numpy as jnp
from jax import lax
from jax.sharding import PartitionSpec as P

norm_eps = 1e-05
moment_eps = 1e-06


def kurtosis_terms(rotated, second, fourth, full_width):
    moment_two = second / full_width + moment_eps
    kurt_vals = fourth / full_width / (moment_two * moment_two)
    cubed = rotated * rotated * rotated
    grad_vals = (
        cubed / (moment_two * moment_two)[:, None] - (kurt_vals / moment_two)[:, None] * rotated
    )
    return (kurt_vals, grad_vals.astype(jnp.bfloat16))


def power_sums(rotated, along):
    squares = rotated * rotated
    return (jnp.sum(squares, axis=along), jnp.sum(squares * squares, axis=along))


def shards(attn_out, residual, w_out, norm_gain, rotation):
    heads_all = lax.all_gather(attn_out, "tok", axis=0, tiled=True)
    row_block = heads_all
    projected = lax.psum_scatter(
        jnp.dot(row_block, w_out, preferred_element_type=jnp.float32),
        "col",
        scatter_dimension=0,
        tiled=True,
    )
    hidden = residual.astype(jnp.float32) + projected
    square_sum = lax.psum(jnp.sum(hidden * hidden, axis=1), "tok")
    full_width = hidden.shape[1] * lax.axis_size("tok")
    row_scale = lax.rsqrt(square_sum / full_width + norm_eps)
    normed = (hidden * row_scale[:, None] * norm_gain[None, :]).astype(jnp.bfloat16)
    normed_all = lax.all_gather(normed, "col", axis=0, tiled=True)
    tokens_total = normed_all.shape[0]
    row_block = normed_all
    rotated = lax.psum_scatter(
        jnp.dot(row_block, rotation, preferred_element_type=jnp.float32),
        "tok",
        scatter_dimension=0,
        tiled=True,
    )
    second, fourth = lax.psum(power_sums(rotated, 1), "col")
    kurt_vals, grad_own = kurtosis_terms(rotated, second, fourth, full_width)
    grad_all = lax.all_gather(grad_own, "tok", axis=0, tiled=True)
    grad_rot = lax.dot_general(
        normed_all, grad_all, (((0,), (0,)), ((), ())), preferred_element_type=jnp.float32
    )
    return (kurt_vals, grad_rot / math.sqrt(tokens_total))


def solution(mesh):
    return jax.shard_map(
        shards,
        mesh=mesh,
        in_specs=(
            P(("groups", "tok"), "col"),
            P(("groups", "col"), "tok"),
            P("col", "tok"),
            P("tok"),
            P("tok", "col"),
        ),
        out_specs=(P(("groups", "tok")), P(("groups", "tok"), "col")),
        check_vma=False,
    )
```

profile of v0, /device:TPU:0, one launch (start us, length us, event | category | flops | bytes accessed | tf_op | source)
XLA Modules:
  0.0 212.4 jit_solution(18247029739795986867)
XLA Ops:
  7.2 0.0 all-gather.4.cloned.1.call-start
  7.2 0.7 all-gather.4.cloned.1.call-update
  7.9 0.0 reduce-scatter.3.cloned.1.call-start
  8.0 32.3 %all-gather.4.cloned.1.call-done = bf16[256,2048]{1,0:T(8,128)(2,1)} async-done(((bf16[64,2048]{1,0:T(8,128)(2,1)}), bf16[256,2048]{1,0:T(8,128)(2,1)}) %all-gather.4.cloned.1.call-update) | async-done | bytes 1048592 | tf_op jit(solution)/shard_map/all_gather | solution.py:27
  40.2 7.4 %fusion.5 = f32[256,2048]{1,0:T(8,128)} fusion(bf16[256,2048]{1,0:T(8,128)(2,1)} %all-gather.4.cloned.1.call-done, bf16[2048,2048]{1,0:T(8,128)(2,1)} %param.7), kind=kOutput, calls=%fused_computation.16 | convolution fusion | flops 2147483648 | bytes 11534336 | tf_op jit(solution)/shard_map/dot_general | solution.py:30
  47.6 0.0 reduce-scatter.3.cloned.1.call-update
  47.6 0.0 all-gather.6.cloned.1.call-start
  47.7 31.0 %reduce-scatter.3.cloned.1.call-done = f32[64,2048]{1,0:T(8,128)} async-done(((f32[256,2048]{1,0:T(8,128)}), f32[64,2048]{1,0:T(8,128)}) %reduce-scatter.3.cloned.1.call-update) | async-done | bytes 524304 | tf_op jit(solution)/shard_map/reduce_scatter | solution.py:29
  78.7 1.2 multiply_reduce_fusion.1
  79.9 11.7 %psum.21 = f32[64]{0:T(128)S(1)} all-reduce(f32[64]{0:T(128)S(1)} %multiply_reduce_fusion.1), channel_id=1, replica_groups=mesh['groups'=2,'tok'=4,'col'=4] {'tok'}, use_global_device_ids=true, to_apply=%region_2.0 | all-reduce | flops 64 | bytes 512 | tf_op jit(solution)/shard_map/psum | solution.py:36
  91.6 1.9 multiply_convert_fusion
  93.5 0.0 all-gather.6.cloned.1.call-update
  93.5 0.0 reduce-scatter.5.cloned.1.call-start
  93.6 14.1 %all-gather.6.cloned.1.call-done = bf16[256,2048]{1,0:T(8,128)(2,1)} async-done(((bf16[64,2048]{1,0:T(8,128)(2,1)}), bf16[256,2048]{1,0:T(8,128)(2,1)}) %all-gather.6.cloned.1.call-update) | async-done | bytes 1048592 | tf_op jit(solution)/shard_map/all_gather | solution.py:40
  107.6 7.4 %fusion.6 = f32[256,2048]{1,0:T(8,128)} fusion(bf16[256,2048]{1,0:T(8,128)(2,1)} %all-gather.6.cloned.1.call-done, bf16[2048,2048]{1,0:T(8,128)(2,1)} %param.9), kind=kOutput, calls=%fused_computation.17 | convolution fusion | flops 2147483648 | bytes 11534336 | tf_op jit(solution)/shard_map/dot_general | solution.py:44
  115.1 0.0 reduce-scatter.5.cloned.1.call-update
  115.1 0.0 all-gather.8.cloned.1.call-start
  115.1 44.0 %reduce-scatter.5.cloned.1.call-done = f32[64,2048]{1,0:T(8,128)} async-done(((f32[256,2048]{1,0:T(8,128)}), f32[64,2048]{1,0:T(8,128)}) %reduce-scatter.5.cloned.1.call-update) | async-done | bytes 524304 | tf_op jit(solution)/shard_map/reduce_scatter | solution.py:43
  159.1 1.2 multiply_reduce_fusion
  160.3 6.4 %all-reduce = (f32[64]{0:T(128)S(1)}, f32[64]{0:T(128)S(1)}) all-reduce(f32[64]{0:T(128)S(1)} %get-tuple-element.3, f32[64]{0:T(128)S(1)} %get-tuple-element.2), channel_id=1, replica_groups=mesh['groups'=2,'tok'=4,'col'=4] {'col'}, use_global_device_ids=true, to_apply=%region_5.0 | all-reduce | flops 128 | bytes 1024 | tf_op jit(solution)/shard_map/psum | solution.py:49
  166.7 0.5 multiply_divide_fusion
  167.2 1.9 fusion.3
  169.2 27.0 %all-gather.8.cloned.1.call-done = bf16[256,2048]{1,0:T(8,128)(2,1)} async-done(((bf16[64,2048]{1,0:T(8,128)(2,1)}), bf16[256,2048]{1,0:T(8,128)(2,1)}) %all-gather.8.cloned.1.call-update) | async-done | bytes 1048592 | tf_op jit(solution)/shard_map/all_gather | solution.py:51
  196.1 9.8 %convolution_multiply_fusion = f32[2048,2048]{1,0:T(8,128)} fusion(bf16[256,2048]{1,0:T(8,128)(2,1)S(1)} %copy-done, bf16[256,2048]{1,0:T(8,128)(2,1)} %all-gather.8.cloned.1.call-done), kind=kOutput, calls=%fused_computation | convolution fusion | flops 2151677952 | bytes 18874368 | tf_op jit(solution)/shard_map/dot_general | solution.py:52
  (8 shorter events, 0.0 us)
Async XLA Ops:
  7.2 33.1 %all-gather.4.cloned.1.call-start = ((), (), s32[]{:S(2)}) async-start(), calls=%async_computation.2 | async-start | bytes 1310720 | tf_op jit(solution)/shard_map/all_gather | solution.py:27
  7.9 70.8 %copy-start.1 = (bf16[64,2048]{1,0:T(8,128)(2,1)S(1)}, bf16[64,2048]{1,0:T(8,128)(2,1)}, u32[]{:S(2)}) copy-start(bf16[64,2048]{1,0:T(8,128)(2,1)} %param.6) | copy-start | bytes 786436
  7.9 83.7 %copy-start.2 = (f32[2048]{0:T(1024)S(1)}, f32[2048]{0:T(1024)}, u32[]{:S(2)}) copy-start(f32[2048]{0:T(1024)} %param.8) | copy-start | bytes 24580
  7.9 70.8 %reduce-scatter.3.cloned.1.call-start = ((), (), s32[]{:S(2)}) async-start(), calls=%async_computation.3 | async-start | bytes 2621440 | tf_op jit(solution)/shard_map/reduce_scatter | solution.py:29
  47.6 60.0 %all-gather.6.cloned.1.call-start = ((), (), s32[]{:S(2)}) async-start(), calls=%async_computation.4 | async-start | bytes 1310720 | tf_op jit(solution)/shard_map/all_gather | solution.py:40
  93.5 65.6 %reduce-scatter.5.cloned.1.call-start = ((), (), s32[]{:S(2)}) async-start(), calls=%async_computation.5 | async-start | bytes 2621440 | tf_op jit(solution)/shard_map/reduce_scatter | solution.py:43
  107.6 88.5 %copy-start = (bf16[256,2048]{1,0:T(8,128)(2,1)S(1)}, bf16[256,2048]{1,0:T(8,128)(2,1)}, u32[]{:S(2)}) copy-start(bf16[256,2048]{1,0:T(8,128)(2,1)} %all-gather.6.cloned.1.call-done) | copy-start | bytes 3145732
  115.1 81.0 %all-gather.8.cloned.1.call-start = ((), (), s32[]{:S(2)}) async-start(), calls=%async_computation.6 | async-start | bytes 1310720 | tf_op jit(solution)/shard_map/all_gather | solution.py:51
Sparse Core Ops, SparseCore 0:
  9.6 30.6 all-gather.3
  47.7 30.9 reduce-scatter.2
  93.6 13.9 all-gather.5
  115.2 43.8 reduce-scatter.4
  169.3 26.7 all-gather.7
where the time goes:
time: 213 us; the launch traced here: 212 us
  waiting for transfers between devices  149 us (70%)
  matrix products  24.6 us (12%)
  blocking collectives  18.1 us (8%)
  between operations  13.8 us (6%)
  other arithmetic  6.69 us (3%)
    reduce_scatter x1, waiting for transfers between devices, shards(): lax.psum_scatter(jnp.dot(row_block, rotation, preferred_element_type=jnp....  44 us
    all_gather x1, waiting for transfers between devices, shards(): heads_all = lax.all_gather(attn_out, 'tok', axis=0, tiled=True)  32.3 us
    reduce_scatter x1, waiting for transfers between devices, shards(): lax.psum_scatter(jnp.dot(row_block, w_out, preferred_element_type=jnp.flo...  31 us
    all_gather x1, waiting for transfers between devices, shards(): grad_all = lax.all_gather(grad_own, 'tok', axis=0, tiled=True)  27 us
    all_gather x1, waiting for transfers between devices, shards(): normed_all = lax.all_gather(normed, 'col', axis=0, tiled=True)  14.1 us
    psum x1, blocking collectives, shards(): square_sum = lax.psum(jnp.sum(hidden * hidden, axis=1), 'tok')  11.7 us
    dot_general x1, matrix products, shards(): lax.dot_general(normed_all, grad_all, (((0,), (0,)), ((), ())), preferred...  9.77 us
    dot_general x1, matrix products, shards(): jnp.dot(row_block, rotation, preferred_element_type=jnp.float32)  7.44 us
  transfers between devices with their start and end apart: 5, of which 5 were waited for; matrix products, arithmetic and copies ran while one was open for 0% of the time, Pallas kernels for 0%

commit v1 on v0

--- a/solution.py
+++ b/solution.py
@@ -6,6 +6,24 @@
 
 norm_eps = 1e-05
 moment_eps = 1e-06
+
+
+def laid_out(pieces, dim):
+    pieces = jnp.moveaxis(pieces, 0, dim)
+    lengths = pieces.shape
+    return pieces.reshape(*lengths[:dim], lengths[dim] * lengths[dim + 1], *lengths[dim + 2 :])
+
+
+def grow_blocks(value, axis):
+    peers = lax.axis_size(axis)
+    tiles = value[None]
+    for level in range(peers.bit_length() - 1):
+        bit = 1 << level
+        other = lax.ppermute(tiles, axis, [(i, i ^ bit) for i in range(peers)])
+        both = jnp.stack([tiles, other])
+        upper = lax.axis_index(axis) >> level & 1
+        tiles = jnp.where(upper == 0, both, both[::-1]).reshape(-1, *value.shape)
+    return tiles
 
 
 def kurtosis_terms(rotated, second, fourth, full_width):
@@ -24,7 +42,7 @@
 
 
 def shards(attn_out, residual, w_out, norm_gain, rotation):
-    heads_all = lax.all_gather(attn_out, "tok", axis=0, tiled=True)
+    heads_all = laid_out(grow_blocks(attn_out, "tok"), 0)
     row_block = heads_all
     projected = lax.psum_scatter(
         jnp.dot(row_block, w_out, preferred_element_type=jnp.float32),

time: 213 us -> 217 us (1.019)
  starting transfers between devices: 0.2 us -> 6.07 us
    all_gather x1 -> x0, waiting for transfers between devices: 32.3 us -> none  [shards(): heads_all = lax.all_gather(attn_out, 'tok', axis=0, tiled=True)]
    ppermute x0 -> x2, waiting for transfers between devices: none -> 29 us  [grow_blocks(): other = lax.ppermute(tiles, axis, [(i, i ^ bit) for i in range(peers)])]
    ppermute x0 -> x2, starting transfers between devices: none -> 5.91 us  [grow_blocks(): other = lax.ppermute(tiles, axis, [(i, i ^ bit) for i in range(peers)])]
  transfers between devices with their start and end apart: 5 -> 6, of which waited for: 5 -> 6; matrix products, arithmetic and copies ran while one was open for 0% -> 0% of each run, Pallas kernels for 0% -> 0%
where the time goes in v1:
time: 217 us
  waiting for transfers between devices  147 us (68%)
  matrix products  24.3 us (11%)
  blocking collectives  18.1 us (8%)
  between operations  13.8 us (6%)
  other arithmetic  8.2 us (4%)
  starting transfers between devices  6.07 us (3%)
    reduce_scatter x1, waiting for transfers between devices, shards(): lax.psum_scatter(jnp.dot(row_block, rotation, preferred_element_type=jnp....  44 us
    reduce_scatter x1, waiting for transfers between devices, shards(): lax.psum_scatter(jnp.dot(row_block, w_out, preferred_element_type=jnp.flo...  32.5 us
    ppermute x2, waiting for transfers between devices, grow_blocks(): other = lax.ppermute(tiles, axis, [(i, i ^ bit) for i in range(peers)])  29 us
    all_gather x1, waiting for transfers between devices, shards(): grad_all = lax.all_gather(grad_own, 'tok', axis=0, tiled=True)  27 us
    all_gather x1, waiting for transfers between devices, shards(): normed_all = lax.all_gather(normed, 'col', axis=0, tiled=True)  14.1 us
    psum x1, blocking collectives, shards(): square_sum = lax.psum(jnp.sum(hidden * hidden, axis=1), 'tok')  11.7 us
    dot_general x1, matrix products, shards(): lax.dot_general(normed_all, grad_all, (((0,), (0,)), ((), ())), preferred...  9.77 us
    dot_general x1, matrix products, shards(): jnp.dot(row_block, rotation, preferred_element_type=jnp.float32)  7.44 us
  transfers between devices with their start and end apart: 6, of which 6 were waited for; matrix products, arithmetic and copies ran while one was open for 0% of the time, Pallas kernels for 0%

profile of v1, /device:TPU:0, one launch (start us, length us, event | category | flops | bytes accessed | tf_op | source)
XLA Modules:
  0.0 217.1 jit_solution(6291237802757774495)
XLA Ops:
  7.2 3.1 %collective-permute-start = (bf16[1,64,2048]{2,1,0:T(8,128)(2,1)}, bf16[1,64,2048]{2,1,0:T(8,128)(2,1)S(1)}, u32[]{:S(2)}, u32[]{:S(2)}) collective-permute-start(bf16[1,64,2048]{2,1,0:T(8,128)(2,1)} %bitcast.17), channel_id=1, source_target_pairs={{0,4},{4,0},{8,12},{12,8},{1,5},{5,1},{9,13},{13,9},{2,6},{6,2},{1... | collective-permute-start | bytes 786440 | tf_op jit(solution)/shard_map/ppermute | solution.py:22
  10.3 6.5 %collective-permute-done = bf16[1,64,2048]{2,1,0:T(8,128)(2,1)S(1)} collective-permute-done((bf16[1,64,2048]{2,1,0:T(8,128)(2,1)}, bf16[1,64,2048]{2,1,0:T(8,128)(2,1)S(1)}, u32[]{:S(2)}, u32[]{:S(2)}) %collective-permute-start) | collective-permute-done | bytes 262176 | tf_op jit(solution)/shard_map/ppermute | solution.py:22
  16.8 1.0 pad_maximum_fusion.1
  17.8 0.1 fusion.5
  18.0 2.8 %collective-permute-start.1 = (bf16[2,64,2048]{2,1,0:T(8,128)(2,1)S(1)}, bf16[2,64,2048]{2,1,0:T(8,128)(2,1)S(1)}, u32[]{:S(2)}, u32[]{:S(2)}) collective-permute-start(bf16[2,64,2048]{2,1,0:T(8,128)(2,1)S(1)} %get-tuple-element.7), channel_id=1, source_target_pairs={{0,8},{4,12},{8,0},{12,4},{1,9},{5,13},{9,1},{13,5},{2,10},{6,14},... | collective-permute-start | bytes 1572872 | tf_op jit(solution)/shard_map/ppermute | solution.py:22
  20.8 22.5 %collective-permute-done.1 = bf16[2,64,2048]{2,1,0:T(8,128)(2,1)S(1)} collective-permute-done((bf16[2,64,2048]{2,1,0:T(8,128)(2,1)S(1)}, bf16[2,64,2048]{2,1,0:T(8,128)(2,1)S(1)}, u32[]{:S(2)}, u32[]{:S(2)}) %collective-permute-start.1) | collective-permute-done | bytes 524320 | tf_op jit(solution)/shard_map/ppermute | solution.py:22
  43.3 0.1 pad_maximum_fusion
  43.4 0.3 reverse_select_fusion
  43.7 7.1 %fusion.7 = f32[256,2048]{1,0:T(8,128)} fusion(bf16[256,2048]{1,0:T(8,128)(2,1)S(1)} %bitcast.15, bf16[2048,2048]{1,0:T(8,128)(2,1)} %param.7), kind=kOutput, calls=%fused_computation.22 | convolution fusion | flops 2147483648 | bytes 11534336 | tf_op jit(solution)/shard_map/dot_general | solution.py:48
  50.8 0.0 all-gather.3.cloned.1.call-start
  50.9 32.5 %reduce-scatter.3.cloned.1.call-done = f32[64,2048]{1,0:T(8,128)} async-done(((f32[256,2048]{1,0:T(8,128)}), f32[64,2048]{1,0:T(8,128)}) %reduce-scatter.3.cloned.1.call-update) | async-done | bytes 524304 | tf_op jit(solution)/shard_map/reduce_scatter | solution.py:47
  83.4 1.2 multiply_reduce_fusion.1
  84.6 11.7 %psum.21 = f32[64]{0:T(128)S(1)} all-reduce(f32[64]{0:T(128)S(1)} %multiply_reduce_fusion.1), channel_id=1, replica_groups=mesh['groups'=2,'tok'=4,'col'=4] {'tok'}, use_global_device_ids=true, to_apply=%region_2.3 | all-reduce | flops 64 | bytes 512 | tf_op jit(solution)/shard_map/psum | solution.py:54
  96.3 1.9 multiply_convert_fusion
  98.2 14.1 %all-gather.3.cloned.1.call-done = bf16[256,2048]{1,0:T(8,128)(2,1)} async-done(((bf16[64,2048]{1,0:T(8,128)(2,1)}), bf16[256,2048]{1,0:T(8,128)(2,1)}) %all-gather.3.cloned.1.call-update) | async-done | bytes 1048592 | tf_op jit(solution)/shard_map/all_gather | solution.py:58
  112.3 7.4 %fusion.8 = f32[256,2048]{1,0:T(8,128)} fusion(bf16[256,2048]{1,0:T(8,128)(2,1)} %all-gather.3.cloned.1.call-done, bf16[2048,2048]{1,0:T(8,128)(2,1)} %param.9), kind=kOutput, calls=%fused_computation.23 | convolution fusion | flops 2147483648 | bytes 11534336 | tf_op jit(solution)/shard_map/dot_general | solution.py:62
  119.7 0.0 all-gather.5.cloned.1.call-start
  119.8 44.0 %reduce-scatter.5.cloned.1.call-done = f32[64,2048]{1,0:T(8,128)} async-done(((f32[256,2048]{1,0:T(8,128)}), f32[64,2048]{1,0:T(8,128)}) %reduce-scatter.5.cloned.1.call-update) | async-done | bytes 524304 | tf_op jit(solution)/shard_map/reduce_scatter | solution.py:61
  163.8 1.2 multiply_reduce_fusion
  165.0 6.4 %all-reduce = (f32[64]{0:T(128)S(1)}, f32[64]{0:T(128)S(1)}) all-reduce(f32[64]{0:T(128)S(1)} %get-tuple-element.3, f32[64]{0:T(128)S(1)} %get-tuple-element.2), channel_id=1, replica_groups=mesh['groups'=2,'tok'=4,'col'=4] {'col'}, use_global_device_ids=true, to_apply=%region_5.6 | all-reduce | flops 128 | bytes 1024 | tf_op jit(solution)/shard_map/psum | solution.py:67
  171.4 0.5 multiply_divide_fusion
  171.9 1.9 fusion.3
  173.8 27.0 %all-gather.5.cloned.1.call-done = bf16[256,2048]{1,0:T(8,128)(2,1)} async-done(((bf16[64,2048]{1,0:T(8,128)(2,1)}), bf16[256,2048]{1,0:T(8,128)(2,1)}) %all-gather.5.cloned.1.call-update) | async-done | bytes 1048592 | tf_op jit(solution)/shard_map/all_gather | solution.py:69
  200.8 9.8 %convolution_multiply_fusion = f32[2048,2048]{1,0:T(8,128)} fusion(bf16[256,2048]{1,0:T(8,128)(2,1)S(1)} %copy-done, bf16[256,2048]{1,0:T(8,128)(2,1)} %all-gather.5.cloned.1.call-done), kind=kOutput, calls=%fused_computation | convolution fusion | flops 2151677952 | bytes 18874368 | tf_op jit(solution)/shard_map/dot_general | solution.py:70
  (13 shorter events, 0.2 us)
Async XLA Ops:
  7.2 76.2 %reduce-scatter.3.cloned.1.call-start = ((), (), s32[]{:S(2)}) async-start(), calls=%async_computation.2 | async-start | bytes 2621440 | tf_op jit(solution)/shard_map/reduce_scatter | solution.py:47
  7.2 9.6 %collective-permute-start = (bf16[1,64,2048]{2,1,0:T(8,128)(2,1)}, bf16[1,64,2048]{2,1,0:T(8,128)(2,1)S(1)}, u32[]{:S(2)}, u32[]{:S(2)}) collective-permute-start(bf16[1,64,2048]{2,1,0:T(8,128)(2,1)} %bitcast.17), channel_id=1, source_target_pairs={{0,4},{4,0},{8,12},{12,8},{1,5},{5,1},{9,13},{13,9},{2,6},{6,2},{1... | collective-permute-start | bytes 786440 | tf_op jit(solution)/shard_map/ppermute | solution.py:22
  18.0 25.3 %collective-permute-start.1 = (bf16[2,64,2048]{2,1,0:T(8,128)(2,1)S(1)}, bf16[2,64,2048]{2,1,0:T(8,128)(2,1)S(1)}, u32[]{:S(2)}, u32[]{:S(2)}) collective-permute-start(bf16[2,64,2048]{2,1,0:T(8,128)(2,1)S(1)} %get-tuple-element.7), channel_id=1, source_target_pairs={{0,8},{4,12},{8,0},{12,4},{1,9},{5,13},{9,1},{13,5},{2,10},{6,14},... | collective-permute-start | bytes 1572872 | tf_op jit(solution)/shard_map/ppermute | solution.py:22
  43.7 39.7 %copy-start.1 = (bf16[64,2048]{1,0:T(8,128)(2,1)S(1)}, bf16[64,2048]{1,0:T(8,128)(2,1)}, u32[]{:S(2)}) copy-start(bf16[64,2048]{1,0:T(8,128)(2,1)} %param.6) | copy-start | bytes 786436
  43.7 52.6 %copy-start.2 = (f32[2048]{0:T(1024)S(1)}, f32[2048]{0:T(1024)}, u32[]{:S(2)}) copy-start(f32[2048]{0:T(1024)} %param.8) | copy-start | bytes 24580
  50.8 61.5 %all-gather.3.cloned.1.call-start = ((), (), s32[]{:S(2)}) async-start(), calls=%async_computation.3 | async-start | bytes 1310720 | tf_op jit(solution)/shard_map/all_gather | solution.py:58
  98.2 65.6 %reduce-scatter.5.cloned.1.call-start = ((), (), s32[]{:S(2)}) async-start(), calls=%async_computation.4 | async-start | bytes 2621440 | tf_op jit(solution)/shard_map/reduce_scatter | solution.py:61
  112.3 88.5 %copy-start = (bf16[256,2048]{1,0:T(8,128)(2,1)S(1)}, bf16[256,2048]{1,0:T(8,128)(2,1)}, u32[]{:S(2)}) copy-start(bf16[256,2048]{1,0:T(8,128)(2,1)} %all-gather.3.cloned.1.call-done) | copy-start | bytes 3145732
  119.7 81.0 %all-gather.5.cloned.1.call-start = ((), (), s32[]{:S(2)}) async-start(), calls=%async_computation.5 | async-start | bytes 1310720 | tf_op jit(solution)/shard_map/all_gather | solution.py:69
Sparse Core Ops, SparseCore 0:
  50.9 32.3 reduce-scatter.2
  98.3 13.9 all-gather.2
  119.9 43.8 reduce-scatter.4
  173.9 26.7 all-gather.4
